TPU v7x, 32 devices: a whole 2x2x4 slice. The times are simulated.
32 devices in a mesh: det: 4 (over z), tm: 8 (over y, x, core).
Axes of the slice: x: 2, y: 2, z: 4, core: 2. Of those that a mesh axis runs over, the one named last changes fastest.
Arguments:
- iterate: float32 [16, 262144], P(None, ('det', 'tm')), may hold values from -6 to 6
- residual: float32 [16, 262144], P(None, ('det', 'tm')), may hold values from -40 to 40
- direction: float32 [16, 262144], P(None, ('det', 'tm')), may hold values from -2.5 to 2.5
- precond: float32 [262144], P(('det', 'tm')), may hold values from 0.02 to 0.12
- patch_ids: int32 [128, 64], P('det', 'tm'), may hold values from 0 to 4095, as said below
- pixel_in: int32 [128, 8192], P('det', 'tm'), may hold values from 0 to 63
- weights: float32 [128, 8192], P('det', 'tm'), may hold values from 0.5 to 1.5
- filter_diag: float32 [128], P('det'), may hold values from 1 to 1.5
- filter_band: float32 [128, 64], P('det'), may hold values from 0.003125 to 0.0075
Outputs:
- new_iterate: float32 [16, 262144], P(None, ('det', 'tm'))
- new_residual: float32 [16, 262144], P(None, ('det', 'tm'))
- new_direction: float32 [16, 262144], P(None, ('det', 'tm'))
Inputs may be any that keep to these rules, and one draw needn't show every extreme that they name: `patch_ids`: the blocks of one device (detectors 32 d0 .. and time blocks 8 t0 .. of its det index a and tm index c) name, for every owner o = a2 * 8 + c2, exactly 8 patches p with p // 128 = o.
All inputs are finite; a program needn't handle non-finite values.
Results may differ from a plain program's by a relative error of at most 0.0003.
Values sent between devices are 32-bit elements; how exact they have to be, the bound alone decides.
A program may use at most 64 MiB of HBM per device.

v0:
```python
import jax
import jax.numpy as jnp
from jax import lax
from jax.sharding import PartitionSpec as P

PX = 64


def with_halo(cells, sides, width):
    for axis, dim in sides:
        count = lax.axis_size(axis)
        ends = count - 1
        head = lax.slice_in_dim(cells, 0, width, axis=dim)
        tail = lax.slice_in_dim(cells, cells.shape[dim] - width, cells.shape[dim], axis=dim)
        cells = jnp.concatenate(
            [
                lax.ppermute(tail, axis, [(i, (i + 1) % count) for i in range(ends)]),
                cells,
                lax.ppermute(head, axis, [((i + 1) % count, i) for i in range(ends)]),
            ],
            axis=dim,
        )
    return cells


def per_device(
    iterate, residual, direction, precond, patch_ids, pixel_in, weights, filter_diag, filter_band
):
    probes = iterate.shape[0]
    det_rows, time_blocks = patch_ids.shape
    samples = pixel_in.shape[1]
    block_len = samples // time_blocks
    half_band = filter_band.shape[1]
    groups = lax.axis_size("det")
    spans = lax.axis_size("tm")
    devices = groups * spans
    blocks = det_rows * time_blocks
    per_owner = blocks // devices
    own_patches = iterate.shape[1] // PX
    width = probes * PX
    local_old = jnp.sum(residual * precond * residual, axis=1)
    norm_old = lax.psum(local_old, ("det", "tm"))
    patch_flat = patch_ids.reshape(blocks)
    owners = patch_flat // own_patches
    sort_order = jnp.argsort(owners, stable=True)
    inverse = jnp.argsort(sort_order, stable=True)
    requests = (patch_flat[sort_order] % own_patches).reshape(devices, per_owner)
    asked_rows = lax.all_to_all(requests, ("det", "tm"), split_axis=0, concat_axis=0, tiled=True)
    asked_hot = (
        asked_rows.reshape(-1)[:, None] == jnp.arange(own_patches, dtype=jnp.int32)[None, :]
    ).astype(jnp.float32)
    patch_table = (
        direction.reshape(probes, own_patches, PX).transpose(1, 0, 2).reshape(own_patches, width)
    )
    served = jnp.dot(asked_hot, patch_table, precision=lax.Precision.HIGHEST).reshape(
        devices, per_owner, width
    )
    fetched = lax.all_to_all(served, ("det", "tm"), split_axis=0, concat_axis=0, tiled=True)
    block_vals = fetched.reshape(blocks, width)[inverse].reshape(blocks, probes, PX)
    pixel_hot = (
        pixel_in.reshape(blocks, block_len)[:, :, None]
        == jnp.arange(PX, dtype=jnp.int32)[None, None, :]
    ).astype(jnp.float32)
    sample_gain = weights.reshape(blocks, block_len)
    timeline = (
        jnp.einsum("bpx,bsx->bps", block_vals, pixel_hot, precision=lax.Precision.HIGHEST)
        * sample_gain[:, None, :]
    )
    timeline = (
        timeline.reshape(det_rows, time_blocks, probes, block_len)
        .transpose(2, 0, 1, 3)
        .reshape(probes, det_rows, samples)
    )
    padded = with_halo(timeline, (("tm", 2),), half_band)
    windows = jnp.concatenate(
        [
            padded[:, :, :samples].reshape(probes, det_rows, time_blocks, block_len),
            padded[:, :, block_len : samples + block_len].reshape(
                probes, det_rows, time_blocks, block_len
            ),
        ],
        axis=3,
    )
    coeffs = jnp.concatenate([filter_diag[:, None], filter_band], axis=1)
    offsets = jnp.abs(
        jnp.arange(2 * block_len, dtype=jnp.int32)[:, None]
        - jnp.arange(block_len, dtype=jnp.int32)[None, :]
        - half_band
    )
    band_hot = (
        offsets[:, :, None] == jnp.arange(half_band + 1, dtype=jnp.int32)[None, None, :]
    ).astype(jnp.float32)
    toeplitz = jnp.einsum("usk,dk->dus", band_hot, coeffs, precision=lax.Precision.HIGHEST)
    filtered = jnp.einsum("pdju,dus->pdjs", windows, toeplitz, precision=lax.Precision.HIGHEST)
    weighted = (
        filtered.transpose(1, 2, 0, 3).reshape(blocks, probes, block_len) * sample_gain[:, None, :]
    )
    partial_value = jnp.einsum(
        "bps,bsx->bpx", weighted, pixel_hot, precision=lax.Precision.HIGHEST
    ).reshape(blocks, width)
    partial_value = partial_value[sort_order].reshape(devices, per_owner, width)
    collected = lax.all_to_all(
        partial_value, ("det", "tm"), split_axis=0, concat_axis=0, tiled=True
    )
    collected = collected.reshape(devices * per_owner, width)
    summed = lax.dot_general(
        asked_hot, collected, (((0,), (0,)), ((), ())), precision=lax.Precision.HIGHEST
    )
    image_map = (
        summed.reshape(own_patches, probes, PX).transpose(1, 0, 2).reshape(probes, own_patches * PX)
    )
    local_curv = jnp.sum(direction * image_map, axis=1)
    curvature = lax.psum(local_curv, ("det", "tm"))
    step_size = norm_old / curvature
    new_iterate = iterate + step_size[:, None] * direction
    new_residual = residual - step_size[:, None] * image_map
    scaled = precond * new_residual
    norm_new = lax.psum(jnp.sum(new_residual * scaled, axis=1), ("det", "tm"))
    new_direction = scaled + (norm_new / norm_old)[:, None] * direction
    return (new_iterate, new_residual, new_direction)


def solution(mesh):
    in_specs = (
        P(None, ("det", "tm")),
        P(None, ("det", "tm")),
        P(None, ("det", "tm")),
        P(("det", "tm")),
        P("det", "tm"),
        P("det", "tm"),
        P("det", "tm"),
        P("det"),
        P("det", None),
    )
    out_specs = (P(None, ("det", "tm")), P(None, ("det", "tm")), P(None, ("det", "tm")))
    return jax.shard_map(
        per_device, mesh=mesh, in_specs=in_specs, out_specs=out_specs, check_vma=False
    )
```

profile of v0, /device:TPU:0, one launch (start us, length us, event | category | flops | bytes accessed | tf_op | source)
XLA Modules:
  0.0 209.9 jit_solution(2585544996662870150)
XLA Ops:
  0.6 0.8 copy.28
  1.5 3.2 %sort.31 = (s32[256]{0:T(256)}, s32[256]{0:T(256)S(1)}) sort(s32[256]{0:T(256)S(1)} %and_select_fusion, s32[256]{0:T(256)S(1)} %iota.36), dimensions={0}, to_apply=%region_2.3 | sort | flops 2048 | bytes 4096 | tf_op jit(solution)/shard_map/jit(argsort)/sort | solution.py:45
  4.7 0.6 copy-done.9
  5.3 1.9 gather_fusion
  7.3 0.6 add_select_fusion
  7.9 7.3 %all-to-all-start = ((s32[32,1,8]{2,1,0:T(1,128)}), s32[32,1,8]{2,1,0:T(1,128)S(1)}, u32[]{:S(2)}, u32[]{:S(2)}) async-start(s32[32,1,8]{2,1,0:T(1,128)} %bitcast), calls=%async_computation | async-start | bytes 32768 | tf_op jit(solution)/shard_map/all_to_all | solution.py:48
  15.2 1.5 reshape.152
  16.7 0.3 copy.31
  17.1 5.2 %all-to-all-done = s32[32,1,8]{2,1,0:T(1,128)S(1)} async-done(((s32[32,1,8]{2,1,0:T(1,128)}), s32[32,1,8]{2,1,0:T(1,128)S(1)}, u32[]{:S(2)}, u32[]{:S(2)}) %all-to-all-start) | async-done | bytes 1056 | tf_op jit(solution)/shard_map/all_to_all | solution.py:48
  22.3 1.6 fusion.18
  23.9 2.6 %all-to-all-start.1 = ((f32[32,8,1024]{2,1,0:T(8,128)}), f32[32,8,1024]{2,1,0:T(8,128)S(1)}, u32[]{:S(2)}, u32[]{:S(2)}) async-start(f32[32,8,1024]{2,1,0:T(8,128)} %fusion.18), calls=%async_computation.1 | async-start | bytes 2097152 | tf_op jit(solution)/shard_map/all_to_all | solution.py:58
  26.6 3.2 %sort.32 = (s32[256]{0:T(256)}, s32[256]{0:T(256)S(1)}) sort(s32[256]{0:T(256)S(1)} %get-tuple-element.5, s32[256]{0:T(256)S(1)} %iota.37), dimensions={0}, to_apply=%region_3.4 | sort | flops 2048 | bytes 4096 | tf_op jit(solution)/shard_map/jit(argsort)/sort | solution.py:46
  29.8 0.7 copy.30
  30.6 22.2 %all-to-all-done.1 = f32[32,8,1024]{2,1,0:T(8,128)S(1)} async-done(((f32[32,8,1024]{2,1,0:T(8,128)}), f32[32,8,1024]{2,1,0:T(8,128)S(1)}, u32[]{:S(2)}, u32[]{:S(2)}) %all-to-all-start.1) | async-done | bytes 1048608 | tf_op jit(solution)/shard_map/all_to_all | solution.py:58
  52.8 1.1 gather_fusion.1
  53.9 0.3 copy.33
  54.2 1.3 copy.34
  55.5 4.2 %fusion.12 = f32[256,16,128]{2,1,0:T(8,128)S(1)} fusion(f32[256,16,64]{2,1,0:T(8,128)S(1)} %copy.34, s32[256,128]{1,0:T(8,128)S(1)} %eq.84, f32[256,128]{1,0:T(8,128)S(1)} %mul.64), kind=kOutput, calls=%fused_computation.21 | convolution fusion | flops 405274624 | bytes 3407872 | tf_op jit(solution)/shard_map/bpx,bsx->bps/dot_general | solution.py:66
  59.8 2.0 copy.53
  61.8 1.7 reshape.157
  63.5 0.1 fusion.27
  63.6 1.3 collective-permute-start
  65.0 1.5 collective-permute-start.1
  66.5 3.8 %fusion.11 = f32[32,256,128,1]{2,0,1,3:T(8,128)S(1)} fusion(s32[256,128]{1,0:T(8,128)S(1)} %add_abs_fusion, f32[32,64]{1,0:T(8,128)S(1)} %copy-done.8, f32[32,1]{1,0:T(8,128)S(1)} %copy-done.7), kind=kOutput, calls=%fused_computation.16 | convolution fusion | flops 820021248 | bytes 4333696 | tf_op jit(solution)/shard_map/usk,dk->dus/dot_general | solution.py:93
  70.3 1.2 pad_maximum_fusion.1
  71.5 0.5 copy.48
  72.0 1.2 copy.36
  73.2 0.5 copy.49
  73.7 1.2 copy.37
  74.9 7.9 %fusion.4 = f32[32,128,16,8]{1,2,3,0:T(8,128)S(1)} fusion(f32[16,32,8,128]{3,0,2,1:T(8,128)S(1)} %copy.37, f32[16,32,8,128]{3,0,2,1:T(8,128)S(1)} %copy.36, f32[32,256,128,1]{2,0,1,3:T(8,128)S(1)} %fusion.11), kind=kOutput, calls=%fused_computation.9 | convolution fusion | flops 1611661312 | bytes 10485760 | tf_op jit(solution)/shard_map/pdju,dus->pdjs/dot_general | solution.py:94
  82.8 0.2 bitcast_multiply_fusion
  83.1 6.6 %fusion.1 = f32[256,16,64]{2,1,0:T(8,128)S(1)} fusion(f32[256,16,128]{2,1,0:T(8,128)S(1)} %bitcast_multiply_fusion, s32[256,128]{1,0:T(8,128)S(1)} %eq.84), kind=kOutput, calls=%fused_computation.6 | convolution fusion | flops 404750336 | bytes 3276800 | tf_op jit(solution)/shard_map/bps,bsx->bpx/dot_general | solution.py:98
  89.7 1.0 copy.39
  90.7 0.3 copy.40
  91.1 2.2 %gather_fusion.2 = f32[256,1024]{1,0:T(8,128)} fusion(f32[256,1024]{1,0:T(8,128)S(1)} %copy.40, s32[1024]{0:T(1024)} %copy-done.9), kind=kCustom, calls=%fused_computation.2 | custom fusion | bytes 2098176 | tf_op jit(solution)/shard_map/gather | solution.py:101
  93.3 7.7 %all-to-all-start.2 = ((f32[32,8,1024]{2,1,0:T(8,128)}), f32[32,8,1024]{2,1,0:T(8,128)S(1)}, u32[]{:S(2)}, u32[]{:S(2)}) async-start(f32[32,8,1024]{2,1,0:T(8,128)} %bitcast.17), calls=%async_computation.2 | async-start | bytes 2097152 | tf_op jit(solution)/shard_map/all_to_all | solution.py:102
  100.9 0.5 broadcast.113
  101.5 0.7 reduce.3
  102.2 24.9 %all-to-all-done.2 = f32[32,8,1024]{2,1,0:T(8,128)S(1)} async-done(((f32[32,8,1024]{2,1,0:T(8,128)}), f32[32,8,1024]{2,1,0:T(8,128)S(1)}, u32[]{:S(2)}, u32[]{:S(2)}) %all-to-all-start.2) | async-done | bytes 1048608 | tf_op jit(solution)/shard_map/all_to_all | solution.py:102
  127.2 0.3 copy.41
  127.6 0.7 convolution_bitcast_fusion
  128.2 0.3 copy.42
  128.6 0.4 reshape.164
  129.0 0.3 fusion.14
  129.2 38.5 %all-reduce = (f32[16]{0:T(128)S(1)}, f32[16]{0:T(128)S(1)}) all-reduce(f32[16]{0:T(128)S(1)} %get-tuple-element.17, f32[16]{0:T(128)S(1)} %get-tuple-element.18), channel_id=1, replica_groups=mesh['det'=4,'tm'=8] {'det','tm'}, use_global_device_ids=true, to_apply=%region_1.0 | all-reduce | flops 32 | bytes 256 | tf_op jit(solution)/shard_map/psum | solution.py:42
  167.7 0.3 fusion.13
  168.0 40.8 %psum.23 = f32[16]{0:T(128)S(1)} all-reduce(f32[16]{0:T(128)S(1)} %get-tuple-element.9), channel_id=1, replica_groups=mesh['det'=4,'tm'=8] {'det','tm'}, use_global_device_ids=true, to_apply=%region_7.8 | all-reduce | flops 16 | bytes 128 | tf_op jit(solution)/shard_map/psum | solution.py:118
  208.8 1.1 multiply_add_fusion
  (38 shorter events, 0.4 us)
Async XLA Ops:
  4.7 0.6 copy-start.9
  7.9 14.4 %all-to-all-start = ((s32[32,1,8]{2,1,0:T(1,128)}), s32[32,1,8]{2,1,0:T(1,128)S(1)}, u32[]{:S(2)}, u32[]{:S(2)}) async-start(s32[32,1,8]{2,1,0:T(1,128)} %bitcast), calls=%async_computation | async-start | bytes 32768 | tf_op jit(solution)/shard_map/all_to_all | solution.py:48
  17.0 12.7 %copy-start.10 = (f32[32]{0:T(128)S(1)}, f32[32]{0:T(128)}, u32[]{:S(2)}) copy-start(f32[32]{0:T(128)} %param.16) | copy-start | bytes 388
  17.0 13.4 %copy-start.5 = (s32[32,1024]{1,0:T(8,128)S(1)}, s32[32,1024]{1,0:T(8,128)}, u32[]{:S(2)}) copy-start(s32[32,1024]{1,0:T(8,128)} %param.14) | copy-start | bytes 393220
  17.1 13.4 %copy-start.6 = (f32[32,1024]{1,0:T(8,128)S(1)}, f32[32,1024]{1,0:T(8,128)}, u32[]{:S(2)}) copy-start(f32[32,1024]{1,0:T(8,128)} %param.15) | copy-start | bytes 393220
  23.9 28.9 %all-to-all-start.1 = ((f32[32,8,1024]{2,1,0:T(8,128)}), f32[32,8,1024]{2,1,0:T(8,128)S(1)}, u32[]{:S(2)}, u32[]{:S(2)}) async-start(f32[32,8,1024]{2,1,0:T(8,128)} %fusion.18), calls=%async_computation.1 | async-start | bytes 2097152 | tf_op jit(solution)/shard_map/all_to_all | solution.py:58
  61.8 4.7 %copy-start.7 = (f32[32,1]{1,0:T(8,128)S(1)}, f32[32,1]{1,0:T(8,128)}, u32[]{:S(2)}) copy-start(f32[32,1]{1,0:T(8,128)} %copy.30) | copy-start | bytes 388
  61.8 4.7 %copy-start.8 = (f32[32,64]{1,0:T(8,128)S(1)}, f32[32,64]{1,0:T(8,128)}, u32[]{:S(2)}) copy-start(f32[32,64]{1,0:T(8,128)} %param.17) | copy-start | bytes 24580
  63.6 6.7 %collective-permute-start = (f32[16,32,64]{2,1,0:T(8,128)S(1)}, f32[16,32,64]{2,1,0:T(8,128)S(1)}, u32[]{:S(2)}, u32[]{:S(2)}) collective-permute-start(f32[16,32,64]{2,1,0:T(8,128)S(1)} %get-tuple-element.13), channel_id=1, source_target_pairs={{0,1},{1,2},{2,3},{3,4},{4,5},{5,6},{6,7},{8,9},{9,10},{10,11},{11... | collective-permute-start | bytes 393224 | tf_op jit(solution)/shard_map/ppermute | solution.py:17
  65.0 5.3 %collective-permute-start.1 = (f32[16,32,64]{2,1,0:T(8,128)S(1)}, f32[16,32,64]{2,1,0:T(8,128)S(1)}, u32[]{:S(2)}, u32[]{:S(2)}) collective-permute-start(f32[16,32,64]{2,1,0:T(8,128)S(1)} %get-tuple-element.14), channel_id=1, source_target_pairs={{1,0},{2,1},{3,2},{4,3},{5,4},{6,5},{7,6},{9,8},{10,9},{11,10},{12... | collective-permute-start | bytes 393224 | tf_op jit(solution)/shard_map/ppermute | solution.py:19
  93.3 33.9 %all-to-all-start.2 = ((f32[32,8,1024]{2,1,0:T(8,128)}), f32[32,8,1024]{2,1,0:T(8,128)S(1)}, u32[]{:S(2)}, u32[]{:S(2)}) async-start(f32[32,8,1024]{2,1,0:T(8,128)} %bitcast.17), calls=%async_computation.2 | async-start | bytes 2097152 | tf_op jit(solution)/shard_map/all_to_all | solution.py:102
  127.5 1.4 copy-start
  127.5 1.4 copy-start.2
  127.5 1.4 copy-start.4
  128.6 80.2 %copy-start.3 = (f32[16,8192]{1,0:T(8,128)S(1)}, f32[16,8192]{1,0:T(8,128)}, u32[]{:S(2)}) copy-start(f32[16,8192]{1,0:T(8,128)} %param.9) | copy-start | bytes 1572868
  168.0 41.9 %copy-start.1 = (f32[16,8192]{1,0:T(8,128)}, f32[16,8192]{1,0:T(8,128)S(1)}, u32[]{:S(2)}) copy-start(f32[16,8192]{1,0:T(8,128)S(1)} %get-tuple-element.10) | copy-start | bytes 1572868
where the time goes:
time: 211 us; the launch traced here: 210 us
  blocking collectives  79.3 us (38%)
  waiting for transfers between devices  52.4 us (25%)
  matrix products  24.9 us (12%)
  local copies, waits for them, and re-layouts  21.1 us (10%)
  starting transfers between devices  20.4 us (10%)
  other arithmetic  10.8 us (5%)
    psum x1, blocking collectives, per_device(): norm_new = lax.psum(jnp.sum(new_residual * scaled, axis=1), ('det', 'tm'))  40.8 us
    psum x1, blocking collectives, per_device(): norm_old = lax.psum(local_old, ('det', 'tm'))  38.5 us
    all_to_all x1, waiting for transfers between devices, per_device(): lax.all_to_all(partial_value, ('det', 'tm'), split_axis=0, concat_axis=0,...  24.9 us
    all_to_all x1, waiting for transfers between devices, per_device(): lax.all_to_all(served, ('det', 'tm'), split_axis=0, concat_axis=0, tiled=...  22.2 us
    dot_general x1, matrix products, per_device(): jnp.einsum('pdju,dus->pdjs', windows, toeplitz, precision=lax.Precision.H...  7.91 us
    all_to_all x1, starting transfers between devices, per_device(): lax.all_to_all(partial_value, ('det', 'tm'), split_axis=0, concat_axis=0,...  7.69 us
    all_to_all x1, starting transfers between devices, per_device(): lax.all_to_all(requests, ('det', 'tm'), split_axis=0, concat_axis=0, tile...  7.3 us
    dot_general x1, matrix products, per_device(): jnp.einsum('bps,bsx->bpx', weighted, pixel_hot, precision=lax.Precision.H...  6.59 us
  transfers between devices with their start and end apart: 5, of which 3 were waited for; matrix products, arithmetic and copies ran while one was open for 5% of the time, Pallas kernels for 0%

commit v1 on v0

--- a/solution.py
+++ b/solution.py
@@ -39,7 +39,7 @@
     own_patches = iterate.shape[1] // PX
     width = probes * PX
     local_old = jnp.sum(residual * precond * residual, axis=1)
-    norm_old = lax.psum(local_old, ("det", "tm"))
+    norm_old = lax.psum(lax.psum(local_old, "tm"), "det")
     patch_flat = patch_ids.reshape(blocks)
     owners = patch_flat // own_patches
     sort_order = jnp.argsort(owners, stable=True)

time: 211 us -> 220 us (1.043)
  blocking collectives: 79.3 us -> 105 us
  waiting for transfers between devices: 52.4 us -> 35.9 us
    psum x1 -> x3, blocking collectives: 38.5 us -> 65.3 us  [the longest x1 39.3 us: per_device(): curvature = lax.psum(local_curv, ('det', 'tm'))]
    all_to_all x1, waiting for transfers between devices: 24.9 us -> 8.4 us  [per_device(): lax.all_to_all(partial_value, ('det', 'tm'), split_axis=0, concat_axis=0,...]
where the time goes in v1:
time: 220 us
  blocking collectives  105 us (48%)
  waiting for transfers between devices  35.9 us (16%)
  matrix products  25.5 us (12%)
  local copies, waits for them, and re-layouts  21.1 us (10%)
  starting transfers between devices  19.8 us (9%)
  other arithmetic  11 us (5%)
    psum x1, blocking collectives, per_device(): norm_new = lax.psum(jnp.sum(new_residual * scaled, axis=1), ('det', 'tm'))  40.2 us
    psum x1, blocking collectives, per_device(): curvature = lax.psum(local_curv, ('det', 'tm'))  39.3 us
    psum x2, blocking collectives, per_device(): norm_old = lax.psum(lax.psum(local_old, 'tm'), 'det')  26 us
    all_to_all x1, waiting for transfers between devices, per_device(): lax.all_to_all(served, ('det', 'tm'), split_axis=0, concat_axis=0, tiled=...  22.2 us
    all_to_all x1, waiting for transfers between devices, per_device(): lax.all_to_all(partial_value, ('det', 'tm'), split_axis=0, concat_axis=0,...  8.4 us
    dot_general x1, matrix products, per_device(): jnp.einsum('pdju,dus->pdjs', windows, toeplitz, precision=lax.Precision.H...  7.91 us
    all_to_all x1, starting transfers between devices, per_device(): lax.all_to_all(requests, ('det', 'tm'), split_axis=0, concat_axis=0, tile...  7.3 us
    all_to_all x1, starting transfers between devices, per_device(): lax.all_to_all(partial_value, ('det', 'tm'), split_axis=0, concat_axis=0,...  7.03 us
  transfers between devices with their start and end apart: 5, of which 3 were waited for; matrix products, arithmetic and copies ran while one was open for 5% of the time, Pallas kernels for 0%

profile of v1, /device:TPU:0, one launch (start us, length us, event | category | flops | bytes accessed | tf_op | source)
XLA Modules:
  0.0 219.7 jit_solution(4566914889885449084)
XLA Ops:
  0.6 0.8 copy.28
  1.5 3.2 %sort.31 = (s32[256]{0:T(256)}, s32[256]{0:T(256)S(1)}) sort(s32[256]{0:T(256)S(1)} %and_select_fusion, s32[256]{0:T(256)S(1)} %iota.36), dimensions={0}, to_apply=%region_3.4 | sort | flops 2048 | bytes 4096 | tf_op jit(solution)/shard_map/jit(argsort)/sort | solution.py:45
  4.7 0.6 copy-done.7
  5.3 1.9 gather_fusion
  7.3 0.6 add_select_fusion
  7.9 7.3 %all-to-all-start = ((s32[32,1,8]{2,1,0:T(1,128)}), s32[32,1,8]{2,1,0:T(1,128)S(1)}, u32[]{:S(2)}, u32[]{:S(2)}) async-start(s32[32,1,8]{2,1,0:T(1,128)} %bitcast), calls=%async_computation | async-start | bytes 32768 | tf_op jit(solution)/shard_map/all_to_all | solution.py:48
  15.2 1.5 reshape.152
  16.7 0.3 copy.31
  17.1 5.2 %all-to-all-done = s32[32,1,8]{2,1,0:T(1,128)S(1)} async-done(((s32[32,1,8]{2,1,0:T(1,128)}), s32[32,1,8]{2,1,0:T(1,128)S(1)}, u32[]{:S(2)}, u32[]{:S(2)}) %all-to-all-start) | async-done | bytes 1056 | tf_op jit(solution)/shard_map/all_to_all | solution.py:48
  22.3 1.6 fusion.18
  23.9 2.6 %all-to-all-start.1 = ((f32[32,8,1024]{2,1,0:T(8,128)}), f32[32,8,1024]{2,1,0:T(8,128)S(1)}, u32[]{:S(2)}, u32[]{:S(2)}) async-start(f32[32,8,1024]{2,1,0:T(8,128)} %fusion.18), calls=%async_computation.1 | async-start | bytes 2097152 | tf_op jit(solution)/shard_map/all_to_all | solution.py:58
  26.6 3.2 %sort.32 = (s32[256]{0:T(256)}, s32[256]{0:T(256)S(1)}) sort(s32[256]{0:T(256)S(1)} %get-tuple-element.5, s32[256]{0:T(256)S(1)} %iota.37), dimensions={0}, to_apply=%region_4.5 | sort | flops 2048 | bytes 4096 | tf_op jit(solution)/shard_map/jit(argsort)/sort | solution.py:46
  29.8 0.7 copy.30
  30.6 22.2 %all-to-all-done.1 = f32[32,8,1024]{2,1,0:T(8,128)S(1)} async-done(((f32[32,8,1024]{2,1,0:T(8,128)}), f32[32,8,1024]{2,1,0:T(8,128)S(1)}, u32[]{:S(2)}, u32[]{:S(2)}) %all-to-all-start.1) | async-done | bytes 1048608 | tf_op jit(solution)/shard_map/all_to_all | solution.py:58
  52.8 1.1 gather_fusion.1
  53.9 0.3 copy.33
  54.2 1.3 copy.34
  55.5 4.2 %fusion.12 = f32[256,16,128]{2,1,0:T(8,128)S(1)} fusion(f32[256,16,64]{2,1,0:T(8,128)S(1)} %copy.34, s32[256,128]{1,0:T(8,128)S(1)} %eq.84, f32[256,128]{1,0:T(8,128)S(1)} %mul.64), kind=kOutput, calls=%fused_computation.21 | convolution fusion | flops 405274624 | bytes 3407872 | tf_op jit(solution)/shard_map/bpx,bsx->bps/dot_general | solution.py:66
  59.8 2.0 copy.53
  61.8 1.7 reshape.157
  63.6 1.3 collective-permute-start
  64.9 1.5 collective-permute-start.1
  66.4 4.5 %fusion.11 = f32[32,256,128,1]{2,0,1,3:T(8,128)S(1)} fusion(s32[256,128]{1,0:T(8,128)S(1)} %add_abs_fusion, f32[32,64]{1,0:T(8,128)} %param.17, f32[32,1]{1,0:T(8,128)} %copy.30), kind=kOutput, calls=%fused_computation.16 | convolution fusion | flops 820021248 | bytes 4333696 | tf_op jit(solution)/shard_map/usk,dk->dus/dot_general | solution.py:93
  70.9 1.2 pad_maximum_fusion.1
  72.2 0.5 copy.48
  72.6 1.2 copy.36
  73.9 0.5 copy.49
  74.3 1.2 copy.37
  75.6 7.9 %fusion.4 = f32[32,128,16,8]{1,2,3,0:T(8,128)S(1)} fusion(f32[16,32,8,128]{3,0,2,1:T(8,128)S(1)} %copy.37, f32[16,32,8,128]{3,0,2,1:T(8,128)S(1)} %copy.36, f32[32,256,128,1]{2,0,1,3:T(8,128)S(1)} %fusion.11), kind=kOutput, calls=%fused_computation.9 | convolution fusion | flops 1611661312 | bytes 10485760 | tf_op jit(solution)/shard_map/pdju,dus->pdjs/dot_general | solution.py:94
  83.5 0.2 bitcast_multiply_fusion
  83.7 6.6 %fusion.1 = f32[256,16,64]{2,1,0:T(8,128)S(1)} fusion(f32[256,16,128]{2,1,0:T(8,128)S(1)} %bitcast_multiply_fusion, s32[256,128]{1,0:T(8,128)S(1)} %eq.84), kind=kOutput, calls=%fused_computation.6 | convolution fusion | flops 404750336 | bytes 3276800 | tf_op jit(solution)/shard_map/bps,bsx->bpx/dot_general | solution.py:98
  90.3 1.0 copy.39
  91.4 0.3 copy.40
  91.7 2.2 gather_fusion.2
  93.9 7.0 %all-to-all-start.2 = ((f32[32,8,1024]{2,1,0:T(8,128)}), f32[32,8,1024]{2,1,0:T(8,128)S(1)}, u32[]{:S(2)}, u32[]{:S(2)}) async-start(f32[32,8,1024]{2,1,0:T(8,128)} %bitcast.17), calls=%async_computation.2 | async-start | bytes 2097152 | tf_op jit(solution)/shard_map/all_to_all | solution.py:102
  101.2 16.3 %psum.28 = f32[16]{0:T(128)S(1)} all-reduce(f32[16]{0:T(128)S(1)} %fusion.14), channel_id=1, replica_groups=mesh['det'=4,'tm'=8] {'tm'}, use_global_device_ids=true, to_apply=%region_1.0 | all-reduce | flops 16 | bytes 128 | tf_op jit(solution)/shard_map/psum | solution.py:42
  117.5 0.5 broadcast.113
  118.0 0.7 reduce.3
  118.8 8.4 %all-to-all-done.2 = f32[32,8,1024]{2,1,0:T(8,128)S(1)} async-done(((f32[32,8,1024]{2,1,0:T(8,128)}), f32[32,8,1024]{2,1,0:T(8,128)S(1)}, u32[]{:S(2)}, u32[]{:S(2)}) %all-to-all-start.2) | async-done | bytes 1048608 | tf_op jit(solution)/shard_map/all_to_all | solution.py:102
  127.2 0.3 copy.41
  127.5 0.7 convolution_bitcast_fusion
  128.2 0.3 copy.42
  128.5 0.4 reshape.164
  129.1 9.7 %psum.29 = f32[16]{0:T(128)S(1)} all-reduce(f32[16]{0:T(128)S(1)} %psum.28), channel_id=1, replica_groups=mesh['det'=4,'tm'=8] {'det'}, use_global_device_ids=true, to_apply=%region_2.0 | all-reduce | flops 16 | bytes 128 | tf_op jit(solution)/shard_map/psum | solution.py:42
  138.8 39.3 %psum.30 = f32[16]{0:T(128)S(1)} all-reduce(f32[16]{0:T(128)S(1)} %multiply_reduce_fusion), channel_id=1, replica_groups=mesh['det'=4,'tm'=8] {'det','tm'}, use_global_device_ids=true, to_apply=%region_6.7 | all-reduce | flops 16 | bytes 128 | tf_op jit(solution)/shard_map/psum | solution.py:113
  178.1 0.3 fusion.13
  178.4 40.2 %psum.31 = f32[16]{0:T(128)S(1)} all-reduce(f32[16]{0:T(128)S(1)} %get-tuple-element.7), channel_id=1, replica_groups=mesh['det'=4,'tm'=8] {'det','tm'}, use_global_device_ids=true, to_apply=%region_8.9 | all-reduce | flops 16 | bytes 128 | tf_op jit(solution)/shard_map/psum | solution.py:118
  218.6 1.1 multiply_add_fusion
  (37 shorter events, 1.0 us)
Async XLA Ops:
  4.7 0.6 copy-start.7
  7.9 14.4 %all-to-all-start = ((s32[32,1,8]{2,1,0:T(1,128)}), s32[32,1,8]{2,1,0:T(1,128)S(1)}, u32[]{:S(2)}, u32[]{:S(2)}) async-start(s32[32,1,8]{2,1,0:T(1,128)} %bitcast), calls=%async_computation | async-start | bytes 32768 | tf_op jit(solution)/shard_map/all_to_all | solution.py:48
  17.0 12.7 %copy-start.8 = (f32[32]{0:T(128)S(1)}, f32[32]{0:T(128)}, u32[]{:S(2)}) copy-start(f32[32]{0:T(128)} %param.16) | copy-start | bytes 388
  17.0 13.4 %copy-start.5 = (s32[32,1024]{1,0:T(8,128)S(1)}, s32[32,1024]{1,0:T(8,128)}, u32[]{:S(2)}) copy-start(s32[32,1024]{1,0:T(8,128)} %param.14) | copy-start | bytes 393220
  17.1 13.4 %copy-start.6 = (f32[32,1024]{1,0:T(8,128)S(1)}, f32[32,1024]{1,0:T(8,128)}, u32[]{:S(2)}) copy-start(f32[32,1024]{1,0:T(8,128)} %param.15) | copy-start | bytes 393220
  23.9 28.9 %all-to-all-start.1 = ((f32[32,8,1024]{2,1,0:T(8,128)}), f32[32,8,1024]{2,1,0:T(8,128)S(1)}, u32[]{:S(2)}, u32[]{:S(2)}) async-start(f32[32,8,1024]{2,1,0:T(8,128)} %fusion.18), calls=%async_computation.1 | async-start | bytes 2097152 | tf_op jit(solution)/shard_map/all_to_all | solution.py:58
  63.6 7.3 %collective-permute-start = (f32[16,32,64]{2,1,0:T(8,128)S(1)}, f32[16,32,64]{2,1,0:T(8,128)S(1)}, u32[]{:S(2)}, u32[]{:S(2)}) collective-permute-start(f32[16,32,64]{2,1,0:T(8,128)S(1)} %get-tuple-element.11), channel_id=1, source_target_pairs={{0,1},{1,2},{2,3},{3,4},{4,5},{5,6},{6,7},{8,9},{9,10},{10,11},{11... | collective-permute-start | bytes 393224 | tf_op jit(solution)/shard_map/ppermute | solution.py:17
  64.9 6.0 %collective-permute-start.1 = (f32[16,32,64]{2,1,0:T(8,128)S(1)}, f32[16,32,64]{2,1,0:T(8,128)S(1)}, u32[]{:S(2)}, u32[]{:S(2)}) collective-permute-start(f32[16,32,64]{2,1,0:T(8,128)S(1)} %get-tuple-element.12), channel_id=1, source_target_pairs={{1,0},{2,1},{3,2},{4,3},{5,4},{6,5},{7,6},{9,8},{10,9},{11,10},{12... | collective-permute-start | bytes 393224 | tf_op jit(solution)/shard_map/ppermute | solution.py:19
  93.9 7.0 %copy-start.1 = (f32[16,8192]{1,0:T(8,128)S(1)}, f32[16,8192]{1,0:T(8,128)}, u32[]{:S(2)}) copy-start(f32[16,8192]{1,0:T(8,128)} %param.10) | copy-start | bytes 1572868
  93.9 7.1 %copy-start.4 = (f32[8192]{0:T(1024)S(1)}, f32[8192]{0:T(1024)}, u32[]{:S(2)}) copy-start(f32[8192]{0:T(1024)} %param.12) | copy-start | bytes 98308
  93.9 33.3 %all-to-all-start.2 = ((f32[32,8,1024]{2,1,0:T(8,128)}), f32[32,8,1024]{2,1,0:T(8,128)S(1)}, u32[]{:S(2)}, u32[]{:S(2)}) async-start(f32[32,8,1024]{2,1,0:T(8,128)} %bitcast.17), calls=%async_computation.2 | async-start | bytes 2097152 | tf_op jit(solution)/shard_map/all_to_all | solution.py:102
  127.5 1.4 copy-start
  128.5 90.1 %copy-start.3 = (f32[16,8192]{1,0:T(8,128)S(1)}, f32[16,8192]{1,0:T(8,128)}, u32[]{:S(2)}) copy-start(f32[16,8192]{1,0:T(8,128)} %param.9) | copy-start | bytes 1572868
  178.4 41.3 %copy-start.2 = (f32[16,8192]{1,0:T(8,128)}, f32[16,8192]{1,0:T(8,128)S(1)}, u32[]{:S(2)}) copy-start(f32[16,8192]{1,0:T(8,128)S(1)} %get-tuple-element.8) | copy-start | bytes 1572868
